TPU v7x, 256 devices: a whole 4x4x8 slice. The times are simulated.
256 devices in a mesh: grp: 8 (over y, core), fsdp: 32 (over x, z).
Axes of the slice: x: 4, y: 4, z: 8, core: 2. Of those that a mesh axis runs over, the one named last changes fastest.
Arguments:
- grad_part: bfloat16 [8, 8, 16, 512, 512], P('grp', None, None, 'fsdp'), may hold values from -4 to 4
- adam_v: float32 [8, 16, 512, 512], P('grp', None, 'fsdp'), may hold values from 5e-07 to 4
- owner_of: int32 [8, 16, 1], P('grp'), may hold values from 0 to 31; in each aligned block of 16 rows (0 to 15, 16 to 31, ..., all dimensions but the last counted through in order) at most 2 rows name the same one
- gram_left: float32 [8, 32, 2, 512, 512], P('grp', 'fsdp'), may hold values from -0.25 to 12
- gram_right: float32 [8, 32, 2, 512, 512], P('grp', 'fsdp'), may hold values from -0.25 to 12
- root_left: bfloat16 [8, 32, 2, 512, 512], P('grp', 'fsdp'), may hold values from -0.1 to 1.2
- root_right: bfloat16 [8, 32, 2, 512, 512], P('grp', 'fsdp'), may hold values from -0.1 to 1.2
Outputs:
- update: bfloat16 [8, 16, 512, 512], P('grp', None, 'fsdp')
- gram_left_new: float32 [8, 32, 2, 512, 512], P('grp', 'fsdp')
- gram_right_new: float32 [8, 32, 2, 512, 512], P('grp', 'fsdp')
Inputs may be any that keep to these rules, and one draw needn't show every extreme that they name: `owner_of`: in each group, no owner is named by more than 2 of the group's 16 blocks, a bound that some block reaches.
All inputs are finite; a program needn't handle non-finite values.
Results may differ from a plain program's by a relative error of at most 0.022.
Values may be sent and summed in bfloat16 or wider, within the bound.
A program may use at most 64 MiB of HBM per device.

v0:
```python
import functools

import jax
import jax.numpy as jnp
from jax import lax
from jax.experimental import pallas as pl
from jax.experimental.pallas import tpu as pltpu
from jax.sharding import PartitionSpec as P

BETA2 = 0.9
EPS_ADAM = 1e-08
EPS_NORM = 1e-06
MESH = pl.DeviceIdType.MESH

NX, NY, NZ = 4, 4, 8
BLOCKS, ROWS, ORDER, SLOTS = 16, 16, 512, 2
PARTS = 4
COLS = ORDER // PARTS
CAPS = (4, 5, 6, 8)
CHUNKS = 2
BACK_ORDER = (4, 3, 5, 2, 6, 1, 7, 0)

T_LIST, T_PLACE, T_OWNED, T_PLANE, T_RANK, T_MINE, T_HELD = 0, 64, 72, 80, 96, 112, 114


def position():
    g = lax.axis_index("grp")
    f = lax.axis_index("fsdp")
    return g, f, g // 2, g % 2, f // NZ, f % NZ


def remote(src, dst, send, recv, device):
    return pltpu.make_async_remote_copy(
        src_ref=src, dst_ref=dst, send_sem=send, recv_sem=recv,
        device_id=device, device_id_type=MESH,
    )


def block_places(owner_ref):
    shape = (BLOCKS, 128)
    row = lax.broadcasted_iota(jnp.int32, shape, 0)
    lane = lax.broadcasted_iota(jnp.int32, shape, 1)
    down = jnp.zeros(shape, jnp.int32)
    across = jnp.zeros(shape, jnp.int32)
    for j in range(BLOCKS):
        down = jnp.where(row == j, owner_ref[j], down)
        across = jnp.where(lane == j, owner_ref[j], across)
    count = lambda same: jnp.sum(jnp.where(same & (lane < row), 1.0, 0.0), axis=1, keepdims=True)
    slot = count(down == across).astype(jnp.int32)
    ranks = count(down % NZ == across % NZ)
    return down, slot, ranks.astype(jnp.int32), jnp.max(ranks, keepdims=True) + 1.0


def index_table(down, slot, rank, me, z):
    shape = (BLOCKS, 128)
    row = lax.broadcasted_iota(jnp.int32, shape, 0)
    lane = lax.broadcasted_iota(jnp.int32, shape, 1)
    plane, line = down % NZ, down // NZ
    here = plane == z
    mine = down == me
    whole = jnp.zeros(shape, jnp.int32)
    for first, size, cond, value in (
        (T_LIST, 64, lambda e: (plane == e // 8) & (rank == e % 8), row),
        (T_PLACE, 8, lambda e: here & (line == e // SLOTS) & (slot == e % SLOTS), rank),
        (T_OWNED, 8, lambda e: here & (rank == e), line * SLOTS + slot),
        (T_PLANE, 16, lambda e: row == e, plane),
        (T_RANK, 16, lambda e: row == e, rank),
        (T_MINE, 2, lambda e: mine & (slot == e), row),
        (T_HELD, 2, lambda e: mine & (slot == e), 1),
    ):
        entry = lane - first
        whole += jnp.where((entry >= 0) & (entry < size) & cond(entry), value, 0)
    return jnp.sum(whole.astype(jnp.float32), axis=0, keepdims=True).astype(jnp.int32)


def pair_kernel(parts_ref, owner_hbm, out_ref, first_ref, tbl_ref, which_hbm,
                owner_ref, which_ref, small_sem, own, other, pair, yrecv, load, loads, own_sem, send, recv, lsend, lrecv, ysend, yrecv_sem):
    g, f, y, c, x, z = position()
    owner_copy = pltpu.make_async_copy(owner_hbm, owner_ref, small_sem.at[0])
    owner_copy.start()
    barrier = pltpu.get_barrier_semaphore()
    for d in range(1, 8):
        pl.semaphore_signal(barrier, inc=1, device_id=((g + d) % 8, f), device_id_type=MESH)
    own_copies = []
    for p in range(PARTS):
        cols = pl.ds(p * COLS, COLS)
        copy = pltpu.make_async_copy(parts_ref.at[:, c, :, :, cols], own.at[p], own_sem.at[p])
        copy.start()
        own_copies.append(copy)
    owner_copy.wait()
    down, slot, rank, most = block_places(owner_ref)
    load[...] = jnp.broadcast_to(most, (8, 128))
    pl.semaphore_wait(barrier, 7)
    copies = []
    for p in range(PARTS):
        cols = pl.ds(p * COLS, COLS)
        copy = remote(parts_ref.at[:, 1 - c, :, :, cols], other.at[p], send.at[p], recv.at[p], (y * 2 + 1 - c, f))
        copy.start()
        copies.append(copy)
    load_copies = []
    for d in range(1, 8):
        copy = remote(load, loads.at[d], lsend.at[d], lrecv.at[d], ((g + d) % 8, f))
        copy.start()
        load_copies.append(copy)
    own_copies[0].wait()
    copies[0].wait_recv()
    pair[...] = own[0] + other[0]
    y_copies = []
    for d in range(1, NY):
        to = (y + d) % NY
        copy = remote(pair.at[to], yrecv.at[d - 1], ysend.at[d - 1], yrecv_sem.at[d - 1], (to * 2 + c, f))
        copy.start()
        y_copies.append(copy)
    tbl_ref[...] = jnp.broadcast_to(index_table(down, slot, rank, f, z), (8, 128))
    for p in range(1, PARTS):
        own_copies[p].wait()
        copies[p].wait_recv()
        out_ref[p - 1] = own[p] + other[p]
    most = load[...]
    for d in range(1, 8):
        load_copies[d - 1].wait_recv()
        most = jnp.maximum(most, loads[d])
    most = jnp.max(most)
    which_ref[0] = sum((most > cap).astype(jnp.int32) for cap in CAPS[:-1])
    which_copy = pltpu.make_async_copy(which_ref, which_hbm, small_sem.at[1])
    which_copy.start()
    for copy in load_copies + copies:
        copy.wait_send()
    total = pair[y].astype(jnp.float32)
    for d in range(NY - 1):
        y_copies[d].wait_recv()
        total = total + yrecv[d].astype(jnp.float32)
    first_ref[...] = total
    which_copy.wait()
    for copy in y_copies:
        copy.wait_send()


def pair_sum(grad_part, owner_ids):
    part = (BLOCKS, ROWS, COLS)
    vmem = pl.BlockSpec(memory_space=pltpu.VMEM)
    hbm = pl.BlockSpec(memory_space=pl.ANY)
    return pl.pallas_call(
        pair_kernel,
        out_shape=(
            jax.ShapeDtypeStruct((PARTS - 1, NY) + part, jnp.bfloat16),
            jax.ShapeDtypeStruct(part, jnp.float32),
            jax.ShapeDtypeStruct((8, 128), jnp.int32),
            jax.ShapeDtypeStruct((1,), jnp.int32),
        ),
        in_specs=[hbm, hbm],
        out_specs=(vmem, vmem, vmem, hbm),
        scratch_shapes=[
            pltpu.SMEM((BLOCKS,), jnp.int32),
            pltpu.SMEM((1,), jnp.int32),
            pltpu.SemaphoreType.DMA((2,)),
            pltpu.VMEM((PARTS, NY) + part, jnp.bfloat16),
            pltpu.VMEM((PARTS, NY) + part, jnp.bfloat16),
            pltpu.VMEM((NY,) + part, jnp.bfloat16),
            pltpu.VMEM((NY - 1,) + part, jnp.bfloat16),
            pltpu.VMEM((8, 128), jnp.float32),
            pltpu.VMEM((8, 8, 128), jnp.float32),
            pltpu.SemaphoreType.DMA((PARTS,)),
            pltpu.SemaphoreType.DMA((PARTS,)),
            pltpu.SemaphoreType.DMA((PARTS,)),
            pltpu.SemaphoreType.DMA((8,)),
            pltpu.SemaphoreType.DMA((8,)),
            pltpu.SemaphoreType.DMA((NY - 1,)),
            pltpu.SemaphoreType.DMA((NY - 1,)),
        ],
        compiler_params=pltpu.CompilerParams(
            collective_id=0, has_side_effects=True, vmem_limit_bytes=60 << 20
        ),
        name="pair_sum",
    )(grad_part, owner_ids)


def step_kernel(cap, tbl_hbm, pairs, first, adam_hbm, gl_hbm, gr_hbm, rl_hbm, rr_hbm,
                upd, gl_out, gr_out0, gr_out1, *scratch):
    scratch = list(scratch)
    take = lambda n: [scratch.pop(0) for _ in range(n)]
    gbf, zsend, zrecv = (take(PARTS) for _ in range(3))
    xret = take(NZ)
    (yown, yrecv, gsum, xsend, xrecv, gmat, dirb, xback, zback, zret, adam, gl, gr, rl, rr,
     gpart, gzrecv, gzsum, gxrecv, tbls,
     lsem, ysem, ysend_sem, yrecv_sem, zsend_sem, zrecv_sem, xsend_sem, xrecv_sem,
     bxsend_sem, bxrecv_sem, bzsend_sem, bzrecv_sem, gsend_sem, grecv_sem, osem) = scratch
    g, f, y, c, x, z = position()
    at_y = lambda i: (i * 2 + c, f)
    at_z = lambda i: (g, x * NZ + i)
    at_x = lambda i: (g, i * NZ + z)
    plus = lambda a, d, n: (a + d) % n
    sends = []

    def start(copy):
        copy.start()
        sends.append(copy)
        return copy

    barrier = pltpu.get_barrier_semaphore()
    partners = (
        [at_y(plus(y, d, NY)) for d in range(1, NY)]
        + [at_z(plus(z, d, NZ)) for d in range(1, NZ)]
        + [at_x(plus(x, d, NX)) for d in range(1, NX)]
    )
    for partner in partners:
        pl.semaphore_signal(barrier, inc=1, device_id=partner, device_id_type=MESH)
    own_copies = []
    copy = pltpu.make_async_copy(first, gsum.at[0], ysem.at[0])
    copy.start()
    own_copies.append(copy)
    for p in range(1, PARTS):
        copy = pltpu.make_async_copy(pairs.at[p - 1, y], yown.at[p - 1], ysem.at[p])
        copy.start()
        own_copies.append(copy)
    big = []
    for i, (src, dst) in enumerate(((adam_hbm.at[0], adam), (rl_hbm.at[0, 0], rl), (rr_hbm.at[0, 0], rr),
                                    (gl_hbm.at[0, 0], gl), (gr_hbm.at[0, 0], gr), (tbl_hbm, tbls))):
        copy = pltpu.make_async_copy(src, dst, lsem.at[i])
        if i not in (3, 4):
            copy.start()
        big.append(copy)

    y_copies = [[] for _ in range(PARTS)]

    def exchange(p):
        for d in range(1, NY):
            to = plus(y, d, NY)
            n = (p - 1) * 3 + d - 1
            y_copies[p].append(start(remote(
                pairs.at[p - 1, to], yrecv.at[p - 1, d - 1], ysend_sem.at[n], yrecv_sem.at[n], at_y(to))))

    z_copies = [[] for _ in range(PARTS)]
    x_copies = [[] for _ in range(PARTS + 1)]

    def tbl(i):
        return tbls[0, i]

    def reduce_part(p):
        own_copies[p].wait()
        for copy in y_copies[p]:
            copy.wait_recv()
        if p == 0:
            gbf[p][...] = gsum[p].astype(jnp.bfloat16)
        else:
            total = yown[p - 1].astype(jnp.float32)
            for d in range(NY - 1):
                total = total + yrecv[p - 1, d].astype(jnp.float32)
            gsum[p] = total
            gbf[p][...] = total.astype(jnp.bfloat16)

        @pl.loop(0, NZ)
        def _(i):
            for k in range(cap):
                zsend[p][i, k] = gbf[p][tbl(T_LIST + i * 8 + k)]
        zrecv[p][z] = zsend[p][z]

    def send_part(p):
        for d in range(1, NZ):
            to = plus(z, d, NZ)
            n = p * 7 + d - 1
            z_copies[p].append(start(remote(
                zsend[p].at[to], zrecv[p].at[z], zsend_sem.at[n], zrecv_sem.at[n], at_z(to))))

    def pass_on(p):
        for copy in z_copies[p]:
            copy.wait_recv()

        for i in range(NX * SLOTS):
            k = tbl(T_PLACE + i)
            for r in range(NZ):
                xsend[p, i // SLOTS, i % SLOTS, r] = zrecv[p][r, k]

        if p < PARTS - 1:
            for d in range(1, NX):
                to = plus(x, d, NX)
                n = p * 3 + d - 1
                x_copies[p].append(start(remote(
                    xsend.at[p, to], xrecv.at[p, x], xsend_sem.at[n], xrecv_sem.at[n], at_x(to))))
        else:
            for s in range(SLOTS):
                for d in range(1, NX):
                    to = plus(x, d, NX)
                    n = (p + s) * 3 + d - 1
                    x_copies[p + s].append(start(remote(
                        xsend.at[p, to, s], xrecv.at[p, x, s], xsend_sem.at[n], xrecv_sem.at[n], at_x(to))))
        xrecv[p, x] = xsend[p, x]

    def apply_roots(p, s):
        block = xrecv[p, :, s].reshape(ORDER, COLS)
        gmat[s, :, p * COLS:(p + 1) * COLS] = block
        left = jnp.dot(rl[s], block, preferred_element_type=jnp.float32).astype(jnp.bfloat16)
        term = jnp.dot(left, rr[s, p * COLS:(p + 1) * COLS, :], preferred_element_type=jnp.float32)
        term = term.reshape(NX, NZ, ROWS, ORDER)
        if p == 0:
            dirb[s] = term
        else:
            dirb[s] += term

    def apply_both(p):
        for copy in x_copies[p]:
            copy.wait_recv()
        pl.loop(0, SLOTS)(lambda s: apply_roots(p, s))

    graft_z = []
    graft_x = []

    def graft_first():
        big[0].wait()
        part = jnp.zeros((BLOCKS, COLS), jnp.float32)
        for p in range(PARTS):
            total = gsum[p]
            second = BETA2 * adam[:, :, p * COLS:(p + 1) * COLS] + (1.0 - BETA2) * total * total
            ratio = total / (jnp.sqrt(second) + EPS_ADAM)
            part = part + jnp.sum(ratio * ratio, axis=1)
        gpart[...] = part
        for d in range(1, NZ):
            graft_z.append(start(remote(
                gpart, gzrecv.at[d - 1], gsend_sem.at[d - 1], grecv_sem.at[d - 1], at_z(plus(z, d, NZ)))))

    def graft_second():
        total = gpart[...]
        for d in range(NZ - 1):
            graft_z[d].wait_recv()
            total = total + gzrecv[d]
        gzsum[...] = total
        for d in range(1, NX):
            n = 6 + d
            graft_x.append(start(remote(
                gzsum, gxrecv.at[d - 1], gsend_sem.at[n], grecv_sem.at[n], at_x(plus(x, d, NX)))))

    big[5].wait()
    reduce_part(0)
    pl.semaphore_wait(barrier, len(partners))
    exchange(1)
    send_part(0)
    for p in range(2, PARTS):
        exchange(p)
    reduce_part(1)
    send_part(1)
    pass_on(0)
    reduce_part(2)
    send_part(2)
    pass_on(1)
    reduce_part(3)
    send_part(3)
    big[3].start()
    big[4].start()
    graft_first()
    big[1].wait()
    big[2].wait()
    apply_both(0)
    pass_on(2)
    graft_second()
    apply_both(1)
    pass_on(3)
    apply_both(2)
    graft = gzsum[...]
    for d in range(NX - 1):
        graft_x[d].wait_recv()
        graft = graft + gxrecv[d]
    block_ids = lax.broadcasted_iota(jnp.int32, (BLOCKS, COLS), 0)
    graft_norms = []
    for s in range(SLOTS):
        graft_norms.append(jnp.sqrt(jnp.sum(jnp.where(block_ids == tbl(T_MINE + s), graft, 0.0), keepdims=True)))
    scales = []
    for s in range(SLOTS):
        for copy in x_copies[PARTS - 1 + s]:
            copy.wait_recv()
        apply_roots(PARTS - 1, s)
        whole = dirb[s]
        norm = jnp.sqrt(jnp.sum((whole * whole).reshape(ORDER, ORDER), keepdims=True))
        scales.append(-(graft_norms[s] / (norm + EPS_NORM)))
    forward = list(sends)
    bx_copies = [[] for _ in range(NZ)]
    bz_copies = []
    for d in BACK_ORDER:
        plane = plus(z, d, NZ)
        for s in range(SLOTS):
            xback[d, :, s] = (dirb[s, :, plane] * scales[s]).astype(jnp.bfloat16)
        for e in range(1, NX):
            to = plus(x, e, NX)
            n = d * 3 + e - 1
            bx_copies[d].append(start(remote(
                xback.at[d, to], xret[d].at[x], bxsend_sem.at[n], bxrecv_sem.at[n], at_x(to))))
        xret[d][x] = xback[d, x]

    big[3].wait()
    big[4].wait()

    def add_grams(s):
        held = tbl(T_HELD + s) > 0
        block = gmat[s]
        outer = lax.dot_general(block, block, (((1,), (1,)), ((), ())), preferred_element_type=jnp.float32)
        gl_out[0, 0, s] = gl[s] + jnp.where(held, outer, 0.0)
        outer = lax.dot_general(block, block, (((0,), (0,)), ((), ())), preferred_element_type=jnp.float32)
        gr[s] = gr[s] + jnp.where(held, outer, 0.0)

    pl.loop(0, SLOTS)(add_grams)
    gr_out0[0, 0, 0] = gr[0]
    out_copy = pltpu.make_async_copy(gr.at[1], gr_out1.at[0, 0, 0], osem)
    out_copy.start()

    for d in BACK_ORDER:
        for copy in bx_copies[d]:
            copy.wait_recv()
        land = zback if d else zret
        for k in range(cap):
            e = tbl(T_OWNED + k)
            land[d, k] = xret[d][e // SLOTS, e % SLOTS]
        if d:
            bz_copies.append(start(remote(
                zback.at[d], zret.at[d], bzsend_sem.at[d - 1], bzrecv_sem.at[d - 1], at_z(plus(z, d, NZ)))))
    for copy in forward:
        copy.wait_send()
    out_copy.wait()
    for copies in bx_copies:
        for copy in copies:
            copy.wait_send()
    for copy in bz_copies:
        copy.wait()
    for j in range(BLOCKS):
        away = (z + NZ - tbl(T_PLANE + j)) % NZ
        upd[0, j] = zret[away, tbl(T_RANK + j)]


def step(cap, collective_id, tbl, pairs, first, adam_v, gram_left, gram_right, root_left, root_right):
    tile = (ROWS, COLS)
    bf, f32 = jnp.bfloat16, jnp.float32
    vm = pltpu.VMEM
    dma = pltpu.SemaphoreType.DMA
    scratch = (
        [vm((BLOCKS,) + tile, bf)] * PARTS
        + [vm((NZ, cap) + tile, bf)] * PARTS
        + [vm((NZ, cap) + tile, bf)] * PARTS
        + [vm((NX, SLOTS, ROWS, ORDER), bf)] * NZ
        + [
            vm((PARTS - 1, BLOCKS) + tile, bf),
            vm((PARTS - 1, NY - 1, BLOCKS) + tile, bf),
            vm((PARTS, BLOCKS) + tile, f32),
            vm((PARTS, NX, SLOTS, NZ) + tile, bf),
            vm((PARTS, NX, SLOTS, NZ) + tile, bf),
            vm((SLOTS, ORDER, ORDER), bf),
            vm((SLOTS, NX, NZ, ROWS, ORDER), f32),
            vm((NZ, NX, SLOTS, ROWS, ORDER), bf),
            vm((NZ, cap, ROWS, ORDER), bf),
            vm((NZ, cap, ROWS, ORDER), bf),
            vm((BLOCKS, ROWS, ORDER), f32),
            vm((SLOTS, ORDER, ORDER), f32),
            vm((SLOTS, ORDER, ORDER), f32),
            vm((SLOTS, ORDER, ORDER), bf),
            vm((SLOTS, ORDER, ORDER), bf),
            vm((BLOCKS, COLS), f32),
            vm((NZ - 1, BLOCKS, COLS), f32),
            vm((BLOCKS, COLS), f32),
            vm((NX - 1, BLOCKS, COLS), f32),
            pltpu.SMEM((8, 128), jnp.int32),
            dma((6,)), dma((PARTS,)),
            dma((PARTS * 3 - 3,)), dma((PARTS * 3 - 3,)),
            dma((PARTS * 7,)), dma((PARTS * 7,)),
            dma((PARTS * 3 + 3,)), dma((PARTS * 3 + 3,)),
            dma((NZ * 3,)), dma((NZ * 3,)),
            dma((NZ - 1,)), dma((NZ - 1,)),
            dma((10,)), dma((10,)), dma,
        ]
    )
    hbm = pl.BlockSpec(memory_space=pl.ANY)
    return pl.pallas_call(
        functools.partial(step_kernel, cap),
        out_shape=(
            pltpu.VMEM((1, BLOCKS, ROWS, ORDER), bf),
            pltpu.VMEM(gram_left.shape, f32),
            pltpu.VMEM((1, 1, 1, ORDER, ORDER), f32),
            jax.ShapeDtypeStruct((1, 1, 1, ORDER, ORDER), f32),
        ),
        in_specs=[hbm] * 8,
        out_specs=(pl.BlockSpec(memory_space=pltpu.VMEM),) * 3 + (hbm,),
        scratch_shapes=scratch,
        compiler_params=pltpu.CompilerParams(
            collective_id=collective_id, has_side_effects=True, vmem_limit_bytes=32 << 20
        ),
        name=f"step_{cap}",
    )(tbl, pairs, first, adam_v, gram_left, gram_right, root_left, root_right)


def place_kernel(upd, gl, gr0, gr1, upd_out, gl_out, gr_out, held, in_sem, sems):
    load = pltpu.make_async_copy(gr1.at[0, 0, 0], held, in_sem)
    load.start()
    pairs = [(gl, gl_out), (gr0.at[0, 0, 0], gr_out.at[0, 0, 0]), (upd, upd_out), (held, gr_out.at[0, 0, 1])]
    copies = []
    for i, (src, dst) in enumerate(pairs):
        if i == 3:
            load.wait()
        copy = pltpu.make_async_copy(src, dst, sems.at[i])
        copy.start()
        copies.append(copy)
    for copy in copies:
        copy.wait()


def place(upd, gl, gr0, gr1):
    hbm = pl.BlockSpec(memory_space=pl.ANY)
    return pl.pallas_call(
        place_kernel,
        out_shape=tuple(jax.ShapeDtypeStruct(a.shape, a.dtype) for a in (upd, gl, gl)),
        in_specs=[hbm] * 4,
        out_specs=(hbm,) * 3,
        scratch_shapes=[
            pltpu.VMEM((ORDER, ORDER), jnp.float32),
            pltpu.SemaphoreType.DMA,
            pltpu.SemaphoreType.DMA((4,)),
        ],
        compiler_params=pltpu.CompilerParams(vmem_limit_bytes=8 << 20),
        name="place",
    )(upd, gl, gr0, gr1)


def per_device(grad_part, adam_v, owner_of, gram_left, gram_right, root_left, root_right):
    by_core = grad_part.reshape((NY, 2) + grad_part.shape[2:])
    pairs, first, table, which = pair_sum(by_core, owner_of.reshape(BLOCKS))
    operands = (table, pairs, first, adam_v, gram_left, gram_right, root_left, root_right)
    branches = [functools.partial(step, cap, i + 1) for i, cap in enumerate(CAPS)]
    return place(*lax.switch(which[0], branches, *operands))


def solution(mesh):
    placed = (
        P("grp", None, None, "fsdp", None),
        P("grp", None, "fsdp", None),
        P("grp", None, None),
        P("grp", "fsdp", None, None, None),
        P("grp", "fsdp", None, None, None),
        P("grp", "fsdp", None, None, None),
        P("grp", "fsdp", None, None, None),
    )
    return jax.shard_map(
        per_device,
        mesh=mesh,
        in_specs=placed,
        out_specs=(
            P("grp", None, "fsdp", None),
            P("grp", "fsdp", None, None, None),
            P("grp", "fsdp", None, None, None),
        ),
        check_vma=False,
    )
```

profile of v0, /device:TPU:4, one launch (start us, length us, event | category | flops | bytes accessed | tf_op | source)
XLA Modules:
  0.0 74.9 jit_solution(10987517987048386745)
XLA Ops:
  0.6 0.0 copy-start
  0.6 11.4 %pair_sum.1 = (bf16[3,4,16,16,128]{4,3,2,1,0:T(8,128)(2,1)}, f32[16,16,128]{2,1,0:T(8,128)S(1)}, s32[8,128]{1,0:T(8,128)S(1)}, s32[1]{0:T(128)}) custom-call(bf16[4,2,16,16,512]{4,3,2,1,0:T(8,128)(2,1)} %bitcast.3, s32[16]{0:T(128)} %bitcast.4), custom_call_target="tpu_custom_call" | custom-call | tf_op jit(solution)/shard_map/pair_sum/pallas_call | solution.py:143
  12.7 0.0 copy-done
  12.7 59.1 %conditional.1 = ((bf16[1,16,16,512]{3,2,1,0:T(8,128)(2,1)S(1)}, f32[1,1,2,512,512]{4,3,2,1,0:T(8,128)S(1)}, f32[1,1,1,512,512]{4,3,2,1,0:T(8,128)S(1)}, f32[1,1,1,512,512]{4,3,2,1,0:T(8,128)})) conditional(s32[]{:T(128)} %bitcast.2, (s32[8,128]{1,0:T(8,128)S(1)}, bf16[3,4,16,16,128]{4,3,2,1,0:T(8,128)(2,1)}, ...), branch_computations={%region_0.0_spmd, %region_1.0_spmd, %region_2.0_spmd, %region_3.0_... | conditional | bytes 8 | solution.py:523
  12.9 58.8 %step_6.1 = (bf16[1,16,16,512]{3,2,1,0:T(8,128)(2,1)S(1)}, f32[1,1,2,512,512]{4,3,2,1,0:T(8,128)S(1)}, f32[1,1,1,512,512]{4,3,2,1,0:T(8,128)S(1)}, f32[1,1,1,512,512]{4,3,2,1,0:T(8,128)}) custom-call(s32[8,128]{1,0:T(8,128)S(1)} %get-tuple-element.80.tbl_hbm, bf16[3,4,16,16,128]{4,3,2,1,0:T(8,128)(2,1)} %get-tuple-element.81.pairs, ...), custom_call_target="tpu_custom_call" | custom-call | tf_op jit(solution)/shard_map/cond/branch_2_fun/step_6/pallas_call | solution.py:468
  71.7 3.0 %place.1 = (bf16[1,16,16,512]{3,2,1,0:T(8,128)(2,1)}, f32[1,1,2,512,512]{4,3,2,1,0:T(8,128)}, f32[1,1,2,512,512]{4,3,2,1,0:T(8,128)}) custom-call(bf16[1,16,16,512]{3,2,1,0:T(8,128)(2,1)S(1)} %get-tuple-element.111.upd, f32[1,1,2,512,512]{4,3,2,1,0:T(8,128)S(1)} %get-tuple-element.112.gl, f32[1,1,1,512,512]{4,3,2,1,0:T(8,128)S(1)} %get-tuple-element.113.gr0, ...), custom_call_target="tpu_custom_call" | custom-call | tf_op jit(solution)/shard_map/place/pallas_call | solution.py:503
Async XLA Ops:
  0.6 12.0 %copy-start = (f32[1,16,16,512]{3,2,1,0:T(8,128)S(1)}, f32[1,16,16,512]{3,2,1,0:T(8,128)}, u32[]{:S(2)}) copy-start(f32[1,16,16,512]{3,2,1,0:T(8,128)} %param.12) | copy-start | bytes 1572868
where the time goes:
time: 75.1 us; the launch traced here: 74.9 us
  Pallas kernels  73.3 us (98%)
  between operations  1.4 us (2%)
    pallas_call x1, Pallas kernels, step(): pl.pallas_call(functools.partial(step_kernel, cap), out_shape=(pltpu.VMEM...  58.8 us
    pallas_call x1, Pallas kernels, pair_sum(): pl.pallas_call(pair_kernel, out_shape=(jax.ShapeDtypeStruct((PARTS - 1, N...  11.4 us
    pallas_call x1, Pallas kernels, place(): pl.pallas_call(place_kernel, out_shape=tuple((jax.ShapeDtypeStruct(a.shap...  3 us

commit v1 on v0

--- a/solution.py
+++ b/solution.py
@@ -253,7 +253,6 @@
         def _(i):
             for k in range(cap):
                 zsend[p][i, k] = gbf[p][tbl(T_LIST + i * 8 + k)]
-        zrecv[p][z] = zsend[p][z]
 
     def send_part(p):
         for d in range(1, NZ):
@@ -261,20 +260,23 @@
             n = p * 7 + d - 1
             z_copies[p].append(start(remote(
                 zsend[p].at[to], zrecv[p].at[z], zsend_sem.at[n], zrecv_sem.at[n], at_z(to))))
+        zrecv[p][z] = zsend[p][z]
 
     def pass_on(p):
         for copy in z_copies[p]:
             copy.wait_recv()
 
-        for i in range(NX * SLOTS):
-            k = tbl(T_PLACE + i)
+        def pick(to, s):
+            k = tbl(T_PLACE + to * SLOTS + s)
             for r in range(NZ):
-                xsend[p, i // SLOTS, i % SLOTS, r] = zrecv[p][r, k]
+                xsend[p, to, s, r] = zrecv[p][r, k]
 
         if p < PARTS - 1:
             for d in range(1, NX):
                 to = plus(x, d, NX)
                 n = p * 3 + d - 1
+                for s in range(SLOTS):
+                    pick(to, s)
                 x_copies[p].append(start(remote(
                     xsend.at[p, to], xrecv.at[p, x], xsend_sem.at[n], xrecv_sem.at[n], at_x(to))))
         else:
@@ -282,8 +284,11 @@
                 for d in range(1, NX):
                     to = plus(x, d, NX)
                     n = (p + s) * 3 + d - 1
+                    pick(to, s)
                     x_copies[p + s].append(start(remote(
                         xsend.at[p, to, s], xrecv.at[p, x, s], xsend_sem.at[n], xrecv_sem.at[n], at_x(to))))
+        for s in range(SLOTS):
+            pick(x, s)
         xrecv[p, x] = xsend[p, x]
 
     def apply_roots(p, s):

time: 75.1 us -> 70.5 us (0.939)
  Pallas kernels: 73.3 us -> 68.5 us
    pallas_call x1, Pallas kernels: 58.8 us -> 54.1 us  [step(): pl.pallas_call(functools.partial(step_kernel, cap), out_shape=(pltpu.VMEM...]
where the time goes in v1:
time: 70.5 us; the launch traced here: 70.4 us
  Pallas kernels  68.5 us (97%)
  between operations  1.4 us (2%)
    pallas_call x1, Pallas kernels, step(): pl.pallas_call(functools.partial(step_kernel, cap), out_shape=(pltpu.VMEM...  54.1 us
    pallas_call x1, Pallas kernels, pair_sum(): pl.pallas_call(pair_kernel, out_shape=(jax.ShapeDtypeStruct((PARTS - 1, N...  11.4 us
    pallas_call x1, Pallas kernels, place(): pl.pallas_call(place_kernel, out_shape=tuple((jax.ShapeDtypeStruct(a.shap...  3 us

profile of v1, /device:TPU:4, one launch (start us, length us, event | category | flops | bytes accessed | tf_op | source)
XLA Modules:
  0.0 70.4 jit_solution(15676897940022117718)
XLA Ops:
  0.6 0.0 copy-start
  0.6 11.4 %pair_sum.1 = (bf16[3,4,16,16,128]{4,3,2,1,0:T(8,128)(2,1)}, f32[16,16,128]{2,1,0:T(8,128)S(1)}, s32[8,128]{1,0:T(8,128)S(1)}, s32[1]{0:T(128)}) custom-call(bf16[4,2,16,16,512]{4,3,2,1,0:T(8,128)(2,1)} %bitcast.3, s32[16]{0:T(128)} %bitcast.4), custom_call_target="tpu_custom_call" | custom-call | tf_op jit(solution)/shard_map/pair_sum/pallas_call | solution.py:143
  12.7 0.0 copy-done
  12.7 54.5 %conditional.1 = ((bf16[1,16,16,512]{3,2,1,0:T(8,128)(2,1)S(1)}, f32[1,1,2,512,512]{4,3,2,1,0:T(8,128)S(1)}, f32[1,1,1,512,512]{4,3,2,1,0:T(8,128)S(1)}, f32[1,1,1,512,512]{4,3,2,1,0:T(8,128)})) conditional(s32[]{:T(128)} %bitcast.2, (s32[8,128]{1,0:T(8,128)S(1)}, bf16[3,4,16,16,128]{4,3,2,1,0:T(8,128)(2,1)}, ...), branch_computations={%region_0.0_spmd, %region_1.0_spmd, %region_2.0_spmd, %region_3.0_... | conditional | bytes 8 | solution.py:528
  12.9 54.1 %step_5.1 = (bf16[1,16,16,512]{3,2,1,0:T(8,128)(2,1)S(1)}, f32[1,1,2,512,512]{4,3,2,1,0:T(8,128)S(1)}, f32[1,1,1,512,512]{4,3,2,1,0:T(8,128)S(1)}, f32[1,1,1,512,512]{4,3,2,1,0:T(8,128)}) custom-call(s32[8,128]{1,0:T(8,128)S(1)} %get-tuple-element.72.tbl_hbm, bf16[3,4,16,16,128]{4,3,2,1,0:T(8,128)(2,1)} %get-tuple-element.73.pairs, ...), custom_call_target="tpu_custom_call" | custom-call | tf_op jit(solution)/shard_map/cond/branch_1_fun/step_5/pallas_call | solution.py:473
  67.2 3.0 %place.1 = (bf16[1,16,16,512]{3,2,1,0:T(8,128)(2,1)}, f32[1,1,2,512,512]{4,3,2,1,0:T(8,128)}, f32[1,1,2,512,512]{4,3,2,1,0:T(8,128)}) custom-call(bf16[1,16,16,512]{3,2,1,0:T(8,128)(2,1)S(1)} %get-tuple-element.111.upd, f32[1,1,2,512,512]{4,3,2,1,0:T(8,128)S(1)} %get-tuple-element.112.gl, f32[1,1,1,512,512]{4,3,2,1,0:T(8,128)S(1)} %get-tuple-element.113.gr0, ...), custom_call_target="tpu_custom_call" | custom-call | tf_op jit(solution)/shard_map/place/pallas_call | solution.py:508
Async XLA Ops:
  0.6 12.0 %copy-start = (f32[1,16,16,512]{3,2,1,0:T(8,128)S(1)}, f32[1,16,16,512]{3,2,1,0:T(8,128)}, u32[]{:S(2)}) copy-start(f32[1,16,16,512]{3,2,1,0:T(8,128)} %param.12) | copy-start | bytes 1572868
